TPU v7x, 128 devices: a whole 4x4x4 slice. The times are simulated.
128 devices in a mesh: morton: 32 (over z, y, core), lane: 4 (over x).
Axes of the slice: x: 4, y: 4, z: 4, core: 2. Of those that a mesh axis runs over, the one named last changes fastest.
Arguments:
- cons_old: float32 [4096, 8, 4096], P(('morton', 'lane')), may hold values from -6 to 6
- flagged: int32 [256], replicated, may hold values from 0 to 4095, as said below
- new_owner: int32 [256], replicated, may hold values from 0 to 127, as said below
- diffusivity: float32 [8], replicated, may hold values from 0.02 to 0.1
- courant: float32 [8], replicated, may hold values from 0.05 to 0.3
Outputs:
- coarse_next: float32 [4096, 8, 4096], P(('morton', 'lane'))
- children: float32 [384, 8, 8, 4096], P(('morton', 'lane'))
Inputs may be any that keep to these rules, and one draw needn't show every extreme that they name: `flagged`: Strictly increasing. The 32 meshblocks of one device hold 0 to 4 flagged parents, some device exactly 4. `new_owner`: Nondecreasing. Each device receives the children of 1 to 3 parents, some device exactly 3. A parent's new owner differs from the device that holds it (flagged // 32) by at most 2, and by exactly 2 in either direction for some parent.
All inputs are finite; a program needn't handle non-finite values.
Results may differ from a plain program's by a relative error of at most 0.000052.
Values sent between devices are 32-bit elements; how exact they have to be, the bound alone decides.
No kernel may reach another device: no remote copies, remote signals or barrier semaphores. Data moves between devices by JAX's collectives and lax.ppermute only.
A program may use at most 192 MiB of HBM per device.

v0:
```python
import functools

import jax
import jax.numpy as jnp
from jax import lax
from jax.experimental import pallas as pl
from jax.experimental.pallas import tpu as pltpu
from jax.sharding import PartitionSpec as P

EDGE = 16
PLANE = EDGE * EDGE
CELLS = EDGE * PLANE
FIELDS = 8
AXES = ("morton", "lane")
CAP = 3
HOLD = 4
EVEN, ODD, WITHIN, ACROSS, HOME = range(5)
ROOM = (2, 1, 1, 1)
RIMS = (EVEN, ODD)
PLACES = [(way, rank) for way in range(HOME) for rank in range(ROOM[way])]
CHUNK = 8


def swaps(count):
    odd = [(i, i + 1) for i in range(1, count - 1, 2)]
    even = [(i, i + 1) for i in range(0, count - 1, 2)]
    across = [(i, i + 2) for i in range(count - 2) if i % 4 >= 2]
    within = [(i, i + 2) for i in range(count - 2) if i % 4 < 2]
    return [pairs + [(b, a) for a, b in pairs] for pairs in (even, odd, within, across)]


def exchange(parts):
    pairs = swaps(lax.axis_size(AXES))
    return [lax.ppermute(part, AXES, pairs[way]) for way, part in enumerate(parts)]


def channel(me, offset):
    near = jnp.where(((me & 1) == 1) == (offset > 0), ODD, EVEN)
    far = jnp.where(((me & 3) >= 2) == (offset > 0), ACROSS, WITHIN)
    return jnp.where(offset == 0, HOME, jnp.where(jnp.abs(offset) == 1, near, far))


def room(way):
    return sum((jnp.where(way == other, count, 0) for other, count in enumerate(ROOM)))


def holder(block, own):
    return block >> (own.bit_length() - 1) if own & (own - 1) == 0 else lax.div(block, jnp.int32(own))


def arrivals(flagged_ref, owner_ref, own, me):
    total = flagged_ref.shape[0]
    start = first_from(owner_ref, total, me)
    sources, found = [], []
    for s in range(CAP):
        place = jnp.minimum(start + s, total - 1)
        block = flagged_ref[place]
        mine = (start + s < total) & (owner_ref[place] == me)
        source = jnp.where(mine, holder(block, own), -1)
        rank = sum(((other == source).astype(jnp.int32) for other in sources), jnp.int32(0))
        sources.append(source)
        found.append((mine, block, channel(me, source - me), rank))
    return found


def first_from(ref, total, bound):
    low = jnp.int32(0)
    for power in reversed(range(total.bit_length())):
        probe = low + (1 << power)
        below = ref[jnp.minimum(probe, total) - 1] < bound
        low = jnp.where((probe <= total) & below, probe, low)
    return low


def rounds_left(flagged, owner, own):
    total = flagged.shape[1]
    rows = (8, total)
    source = jnp.broadcast_to(holder(flagged, own), rows)
    owner = jnp.broadcast_to(owner, rows)
    way = channel(source, owner - source)
    left = jnp.zeros(rows, jnp.int32)
    for rank in range(1, CAP):
        same = (pltpu.roll(source, total - rank, 1) == source) & (pltpu.roll(owner, total - rank, 1) == owner)
        left = jnp.maximum(left, jnp.where(same & (way < HOME), rank + 1 - room(way), 0))
    return jnp.max(left.astype(jnp.float32)).astype(jnp.int32)


def pack_kernel(later, *refs):
    if later:
        turn_ref, *refs = refs
    flagged_ref, owner_ref, cons_ref, *outs, sem = refs
    own = cons_ref.shape[0]
    total = flagged_ref.shape[0]
    me = lax.axis_index(AXES)
    rims = []
    if not later:
        last_plane = cons_ref.at[own - 1, :, pl.ds(CELLS - PLANE, PLANE)]
        first_plane = cons_ref.at[0, :, pl.ds(0, PLANE)]
        for c, way in enumerate(RIMS):
            target = outs[way].at[:, pl.ds(ROOM[way] * CELLS, PLANE)]
            rims.append(pltpu.make_async_copy(first_plane, target, sem.at[HOLD + c]))
            ahead = (me & 1) == c

            @pl.when(ahead)
            def _():
                pltpu.make_async_copy(last_plane, target, sem.at[HOLD + c]).start()

            @pl.when(jnp.logical_not(ahead))
            def _():
                pltpu.make_async_copy(first_plane, target, sem.at[HOLD + c]).start()

    start = first_from(flagged_ref, total, me * own)
    offsets, sent = [], []
    for k in range(HOLD):
        place = jnp.minimum(start + k, total - 1)
        block = flagged_ref[place] - me * own
        mine = (start + k < total) & (block < own)
        block = jnp.clip(block, 0, own - 1)
        offset = owner_ref[place] - me
        rank = sum(((other == offset).astype(jnp.int32) for other in offsets), jnp.int32(0))
        offsets.append(jnp.where(mine, offset, total))
        way = channel(me, offset)
        if later:
            fits = [(c, 0, mine & (way == c) & (rank == room(way) + turn_ref[0])) for c in range(HOME)]
        else:
            fits = [(c, r, mine & (way == c) & (rank == r)) for c, r in PLACES]
        for c, r, fit in fits:

            @pl.when(fit)
            def _():
                pltpu.make_async_copy(cons_ref.at[block], outs[c].at[:, pl.ds(r * CELLS, CELLS)], sem.at[k]).start()

        sent.append(functools.reduce(jnp.logical_or, [fit for _, _, fit in fits]))

    for k in range(HOLD):

        @pl.when(sent[k])
        def _():
            pltpu.make_async_copy(cons_ref.at[0], outs[0].at[:, pl.ds(0, CELLS)], sem.at[k]).wait()

    for copy in rims:
        copy.wait()


def pack(flagged, owner, cons, turn=None):
    fields = cons.shape[1]
    later = turn is not None
    widths = [CELLS] * HOME if later else [ROOM[way] * CELLS + (PLANE if way in RIMS else 0) for way in range(HOME)]
    smem = pl.BlockSpec(memory_space=pltpu.SMEM)
    anywhere = pl.BlockSpec(memory_space=pl.ANY)
    operands = ([turn] if later else []) + [flagged, owner, cons]
    return pl.pallas_call(
        functools.partial(pack_kernel, later),
        out_shape=[jax.ShapeDtypeStruct((fields, width), jnp.float32) for width in widths],
        in_specs=[smem] * (len(operands) - 1) + [anywhere],
        out_specs=[anywhere] * len(widths),
        scratch_shapes=[pltpu.SemaphoreType.DMA((HOLD + 2,))],
        compiler_params=pltpu.CompilerParams(vmem_limit_bytes=1 << 20),
        cost_estimate=pl.CostEstimate(flops=0, bytes_accessed=1 << 20, transcendentals=0),
        name="pack",
    )(*operands)


def by_field(ref, fields):
    rows = lax.broadcasted_iota(jnp.int32, (fields, PLANE), 0)
    value = jnp.zeros((fields, PLANE), jnp.float32)
    for f in range(fields):
        value = jnp.where(rows == f, ref[f], value)
    return value


def split(value):
    high = value.astype(jnp.bfloat16)
    return jnp.concatenate([high, (value - high.astype(jnp.float32)).astype(jnp.bfloat16)], 0)


def dot_split(parts, table):
    product = jnp.dot(parts, table, preferred_element_type=jnp.float32)
    half = parts.shape[0] // 2
    return product[:half] + product[half:]


def beside_table():
    rows = lax.broadcasted_iota(jnp.int32, (PLANE, PLANE), 0)
    columns = lax.broadcasted_iota(jnp.int32, (PLANE, PLANE), 1)
    apart = rows ^ columns
    along_y, along_z = (rows >> 4) - (columns >> 4) & 15, (rows & 15) - (columns & 15) & 15
    same_y, same_z = apart < EDGE, (apart & 15) == 0
    hit = same_z & ((along_y == 1) | (along_y == 15)) | same_y & ((along_z == 1) | (along_z == 15))
    return jnp.where(hit, 1.0, 0.0).astype(jnp.bfloat16)


def refine_values(fine, coarse):
    centre = fine >> 1
    low, high = jnp.maximum(centre - 1, 0), jnp.minimum(centre + 1, EDGE - 1)
    quarter = jnp.where(high - low == 1, 0.25, 0.125) * jnp.where((fine & 1) == 1, 1.0, -1.0)
    slope = jnp.where(coarse == high, quarter, 0.0) - jnp.where(coarse == low, quarter, 0.0)
    return slope + jnp.where(coarse == centre, 1.0, 0.0)


def refine_quarter(q):
    rows = lax.broadcasted_iota(jnp.int32, (PLANE, PLANE), 0)
    columns = lax.broadcasted_iota(jnp.int32, (PLANE, PLANE), 1)
    along_y = refine_values((q >> 1) * EDGE + (columns >> 4), rows >> 4)
    along_z = refine_values((q & 1) * EDGE + (columns & 15), rows & 15)
    return (along_y * along_z).astype(jnp.bfloat16)


def coarse_kernel(*refs):
    scalars, (flagged_hbm, owner_hbm, cons_hbm, out_ref, edge_ref, table_ref, home_ref, plan_ref, left_hbm), refs = refs[:4], refs[4:13], refs[13:]
    copies, (left_ref, flagged_row, owner_row, cons_ref, next_ref, sem, few) = refs[:4], refs[4:]
    flagged_ref, owner_ref, diff_ref, cour_ref = copies
    own, fields, _ = cons_ref.shape
    turns = own // CHUNK
    me = lax.axis_index(AXES)

    loads = 2 * turns
    part = own // loads

    def load(i):
        span = pl.ds(pl.multiple_of(i * part, part), part)
        return pltpu.make_async_copy(cons_hbm.at[span], cons_ref.at[span], sem.at[turns + i])

    few_copies = [pltpu.make_async_copy(*pair, few.at[i]) for i, pair in enumerate(zip((*scalars, flagged_hbm, owner_hbm), (*copies, flagged_row, owner_row)))]
    for copy in few_copies:
        copy.start()
    for i in range(loads):
        load(i).start()
    beside = beside_table()
    for copy in few_copies:
        copy.wait()
    left_ref[0] = rounds_left(flagged_row[...], owner_row[...], own)
    left_copy = pltpu.make_async_copy(left_ref, left_hbm, few.at[len(few_copies)])
    left_copy.start()
    diffuse = by_field(diff_ref, fields)
    courant = by_field(cour_ref, fields)
    centre = 1.0 - 6.0 * diffuse - courant
    back = diffuse + courant
    edge_ref[2] = diffuse
    edge_ref[3] = back

    def store(turn):
        span = pl.ds(pl.multiple_of(turn * CHUNK, CHUNK), CHUNK)
        return pltpu.make_async_copy(next_ref.at[span], out_ref.at[span], sem.at[turn])

    @pl.loop(0, turns)
    def _(turn):
        base = turn * CHUNK

        @pl.when(turn == 0)
        def _():
            load(0).wait()

        load(2 * turn + 1).wait()

        @pl.when(turn < turns - 1)
        def _():
            load(2 * turn + 2).wait()

        places = [(b, x) for b in range(CHUNK) for x in range(EDGE)]
        planes = [cons_ref[base + b, :, pl.ds(x * PLANE, PLANE)] for b, x in places]
        ring = dot_split(split(jnp.concatenate(planes, 0)), beside)
        low = cons_ref[jnp.maximum(base - 1, 0), :, pl.ds(CELLS - PLANE, PLANE)]
        high = cons_ref[jnp.minimum(base + CHUNK, own - 1), :, pl.ds(0, PLANE)]
        low = jnp.where(turn > 0, low, 0.0)
        high = jnp.where(turn < turns - 1, high, 0.0)
        padded = [low] + planes + [high]
        for i, (b, x) in enumerate(places):
            sides = padded[i + 2] + ring[i * fields : (i + 1) * fields]
            next_ref[base + b, :, pl.ds(x * PLANE, PLANE)] = centre * padded[i + 1] + back * padded[i] + diffuse * sides
        store(turn).start()

    for q in range(4):
        table_ref[:, pl.ds(q * PLANE, PLANE)] = refine_quarter(q)

    found = arrivals(flagged_ref, owner_ref, own, me)
    for s, (mine, _, way, rank) in enumerate(found):
        for i, (c, r) in enumerate(PLACES):
            comes = mine & (way == c) & (rank == r)
            plan_ref[s, i] = jnp.full(plan_ref.shape[2:], comes.astype(jnp.int32))

    for s, (mine, block, way, _) in enumerate(found):
        stays = mine & (way == HOME)

        @pl.when(stays)
        def _():
            home_ref[s] = cons_ref[jnp.clip(block - me * own, 0, own - 1)]

        @pl.when(jnp.logical_not(stays))
        def _():
            home_ref[s] = jnp.zeros(home_ref.shape[1:], jnp.float32)

    edge_ref[0] = next_ref[0, :, pl.ds(0, PLANE)]
    edge_ref[1] = next_ref[own - 1, :, pl.ds(CELLS - PLANE, PLANE)]
    for turn in range(turns):
        store(turn).wait()
    left_copy.wait()


def coarse(flagged, owner, diffusivity, courant, cons):
    own, fields, cells = cons.shape
    vmem = pl.BlockSpec(memory_space=pltpu.VMEM)
    hbm = pl.BlockSpec(memory_space=pltpu.HBM)
    return pl.pallas_call(
        coarse_kernel,
        out_shape=[
            pltpu.HBM(cons.shape, jnp.float32),
            jax.ShapeDtypeStruct((4, fields, PLANE), jnp.float32),
            jax.ShapeDtypeStruct((PLANE, 4 * PLANE), jnp.bfloat16),
            jax.ShapeDtypeStruct((CAP, fields, cells), jnp.float32),
            jax.ShapeDtypeStruct((CAP, len(PLACES), fields, 128), jnp.int32),
            pltpu.HBM((1,), jnp.int32),
        ],
        in_specs=[hbm] * 7,
        out_specs=[hbm, vmem, vmem, vmem, vmem, hbm],
        scratch_shapes=[
            *(pltpu.SMEM(value.shape, value.dtype) for value in (flagged, owner, diffusivity, courant)),
            pltpu.SMEM((1,), jnp.int32),
            pltpu.VMEM((1, flagged.shape[0]), jnp.int32),
            pltpu.VMEM((1, owner.shape[0]), jnp.int32),
            pltpu.VMEM(cons.shape, jnp.float32),
            pltpu.VMEM(cons.shape, jnp.float32),
            pltpu.SemaphoreType.DMA((3 * (own // CHUNK),)),
            pltpu.SemaphoreType.DMA((7,)),
        ],
        compiler_params=pltpu.CompilerParams(vmem_limit_bytes=20 << 20),
        cost_estimate=pl.CostEstimate(flops=2 * 2 * own * EDGE * fields * PLANE * PLANE, bytes_accessed=8 << 20, transcendentals=0),
        name="coarse",
    )(
        *(pltpu.with_memory_space_constraint(value, pltpu.HBM) for value in (flagged, owner, diffusivity, courant)),
        *(pltpu.with_memory_space_constraint(value.reshape(1, -1), pltpu.HBM) for value in (flagged, owner)),
        pltpu.with_memory_space_constraint(cons, pltpu.HBM),
    )


def collect_kernel(own, turn_ref, flagged_ref, owner_ref, *refs):
    *parts, _, home_ref = refs
    me = lax.axis_index(AXES)
    for s, (mine, _, way, rank) in enumerate(arrivals(flagged_ref, owner_ref, own, me)):
        for c, part in enumerate(parts):

            @pl.when(mine & (way == c) & (rank == room(way) + turn_ref[0]))
            def _():
                home_ref[s] = part[...]


def collect(own, turn, flagged, owner, parts, home):
    smem = pl.BlockSpec(memory_space=pltpu.SMEM)
    vmem = pl.BlockSpec(memory_space=pltpu.VMEM)
    return pl.pallas_call(
        functools.partial(collect_kernel, own),
        out_shape=jax.ShapeDtypeStruct(home.shape, jnp.float32),
        in_specs=[smem] * 3 + [vmem] * (HOME + 1),
        out_specs=vmem,
        input_output_aliases={3 + HOME: 0},
        compiler_params=pltpu.CompilerParams(vmem_limit_bytes=8 << 20),
        name="collect",
    )(turn, flagged, owner, *parts, home)


def unpack_kernel(plan_ref, *refs):
    parts, (home_ref, edge_ref, table_ref, _, coarse_ref, children_ref, child_ref, rim_ref, sem) = refs[:HOME], refs[HOME:]
    own, fields, _ = coarse_ref.shape
    me = lax.axis_index(AXES)
    rims = [parts[way][:, pl.ds(ROOM[way] * CELLS, PLANE)] for way in RIMS]
    odd = (me & 1) == 1
    rim_ref[0] = edge_ref[0] + edge_ref[3] * jnp.where(odd, rims[0], rims[1])
    rim_ref[1] = edge_ref[1] + edge_ref[2] * jnp.where(odd, rims[1], rims[0])
    spots = (coarse_ref.at[0, :, pl.ds(0, PLANE)], coarse_ref.at[own - 1, :, pl.ds(CELLS - PLANE, PLANE)])
    ends = [pltpu.make_async_copy(rim_ref.at[c], spots[c], sem.at[CAP * 8 + c]) for c in range(2)]
    for copy in ends:
        copy.start()

    def store(s, child):
        return pltpu.make_async_copy(child_ref.at[s, child], children_ref.at[s, child], sem.at[s * 8 + child])

    @pl.loop(0, CAP)
    def _(s):
        comes = [plan_ref[s, i] != 0 for i in range(len(PLACES))]
        planes = []
        for x in range(EDGE):
            halves = []
            for column in range(x * PLANE, (x + 1) * PLANE, 128):
                value = home_ref[s, :, pl.ds(column, 128)]
                for i, (c, r) in enumerate(PLACES):
                    value = jnp.where(comes[i], parts[c][:, pl.ds(r * CELLS + column, 128)], value)
                halves.append(value)
            planes.append(jnp.concatenate(halves, 1))
        parent = split(jnp.concatenate(planes, 0))
        for q in range(4):
            fine = dot_split(parent, table_ref[:, pl.ds(q * PLANE, PLANE)])
            rows = [fine[x * fields : (x + 1) * fields] for x in range(EDGE)]
            for x in range(EDGE):
                low, high = max(x - 1, 0), min(x + 1, EDGE - 1)
                slope = (rows[high] - rows[low]) * (0.25 / (high - low))
                half, place = divmod(2 * x, EDGE)
                child_ref[s, half * 4 + q, :, pl.ds(place * PLANE, PLANE)] = rows[x] - slope
                child_ref[s, half * 4 + q, :, pl.ds((place + 1) * PLANE, PLANE)] = rows[x] + slope
            for half in range(2):
                store(s, half * 4 + q).start()

    @pl.loop(0, CAP * 8)
    def _(i):
        store(i >> 3, i & 7).wait()

    for copy in ends:
        copy.wait()


def unpack(plan, parts, home, edges, table, stepped):
    fields = stepped.shape[1]
    vmem = pl.BlockSpec(memory_space=pltpu.VMEM)
    hbm = pl.BlockSpec(memory_space=pltpu.HBM)
    family = pltpu.HBM((CAP, 8, fields, CELLS), jnp.float32)
    return pl.pallas_call(
        unpack_kernel,
        out_shape=[pltpu.HBM(stepped.shape, jnp.float32), family],
        in_specs=[vmem] * (HOME + 4) + [hbm],
        out_specs=[hbm, hbm],
        scratch_shapes=[
            pltpu.VMEM(family.shape, jnp.float32),
            pltpu.VMEM((2, fields, PLANE), jnp.float32),
            pltpu.SemaphoreType.DMA((CAP * 8 + 2,)),
        ],
        input_output_aliases={HOME + 4: 0},
        compiler_params=pltpu.CompilerParams(vmem_limit_bytes=24 << 20),
        cost_estimate=pl.CostEstimate(flops=2 * 2 * CAP * EDGE * fields * PLANE * 4 * PLANE, bytes_accessed=5 << 20, transcendentals=0),
        name="unpack",
    )(plan, *parts, home, edges, table, stepped)


def shards(cons_old, flagged, new_owner, diffusivity, courant):
    own = cons_old.shape[0]
    arrived = exchange(pack(flagged, new_owner, cons_old))
    stepped, edges, table, home, plan, left = coarse(flagged, new_owner, diffusivity, courant, cons_old)
    left = jnp.maximum(left.reshape(()), 0)

    def later(carry):
        turn, home = carry
        at = turn.reshape((1,))
        parts = exchange(pack(flagged, new_owner, cons_old, at))
        return turn + 1, collect(own, at, flagged, new_owner, parts, home)

    home, arrived = lax.optimization_barrier((home, arrived))
    _, home = lax.while_loop(lambda carry: carry[0] < left, later, (jnp.int32(0), home))
    return tuple(unpack(plan, arrived, home, edges, table, stepped))


def solution(mesh):
    in_specs = (P(AXES, None, None), P(), P(), P(), P())
    out_specs = (P(AXES, None, None), P(AXES, None, None, None))
    return jax.shard_map(shards, mesh=mesh, in_specs=in_specs, out_specs=out_specs, check_vma=False)
```

profile of v0, /device:TPU:97, one launch (start us, length us, event | category | flops | bytes accessed | tf_op | source)
XLA Modules:
  0.0 23.4 jit_solution(3431845035476767956)
XLA Ops:
  0.6 0.0 copy-start.1
  0.6 0.0 copy-start
  0.7 1.6 %pack.2 = (f32[8,8448]{1,0:T(8,128)S(1)}, f32[8,4352]{1,0:T(8,128)S(1)}, f32[8,4096]{1,0:T(8,128)S(1)}, f32[8,4096]{1,0:T(8,128)S(1)}) custom-call(s32[256]{0:T(256)} %refs_0_.3, s32[256]{0:T(256)} %refs_1_.3, f32[32,8,4096]{2,1,0:T(8,128)} %refs_2_.3), custom_call_target="tpu_custom_call" | custom-call | bytes 1048576 | tf_op jit(solution)/shard_map/pack/pallas_call | solution.py:152
  2.3 1.3 %collective-permute-start.4 = (f32[8,8448]{1,0:T(8,128)S(1)}, f32[8,8448]{1,0:T(8,128)S(1)}, u32[]{:S(2)}, u32[]{:S(2)}) collective-permute-start(f32[8,8448]{1,0:T(8,128)S(1)} %get-tuple-element.56), channel_id=1, source_target_pairs={{0,1},{2,3},{4,5},{6,7},{8,9},{10,11},{12,13},{14,15},{16,17},{18,... | collective-permute-start | bytes 811016 | tf_op jit(solution)/shard_map/ppermute | solution.py:34
  3.6 4.6 %collective-permute-start.5 = (f32[8,4352]{1,0:T(8,128)S(1)}, f32[8,4352]{1,0:T(8,128)S(1)}, u32[]{:S(2)}, u32[]{:S(2)}) collective-permute-start(f32[8,4352]{1,0:T(8,128)S(1)} %get-tuple-element.57), channel_id=1, source_target_pairs={{1,2},{3,4},{5,6},{7,8},{9,10},{11,12},{13,14},{15,16},{17,18},{19... | collective-permute-start | bytes 417800 | tf_op jit(solution)/shard_map/ppermute | solution.py:34
  8.1 0.1 collective-permute-start.6
  8.2 7.3 %collective-permute-start.7 = (f32[8,4096]{1,0:T(8,128)S(1)}, f32[8,4096]{1,0:T(8,128)S(1)}, u32[]{:S(2)}, u32[]{:S(2)}) collective-permute-start(f32[8,4096]{1,0:T(8,128)S(1)} %get-tuple-element.59), channel_id=1, source_target_pairs={{2,4},{3,5},{6,8},{7,9},{10,12},{11,13},{14,16},{15,17},{18,20},{1... | collective-permute-start | bytes 393224 | tf_op jit(solution)/shard_map/ppermute | solution.py:34
  15.5 5.0 %coarse.1 = (f32[32,8,4096]{2,1,0:T(8,128)}, f32[4,8,256]{2,1,0:T(8,128)S(1)}, bf16[256,1024]{1,0:T(8,128)(2,1)S(1)}, f32[3,8,4096]{2,1,0:T(8,128)S(1)}, s32[3,5,8,128]{3,2,1,0:T(8,128)S(1)}, /*index=5*/s32[1]{0:T(128)}) custom-call(s32[256]{0:T(256)} %refs_0_.3, s32[256]{0:T(256)} %refs_1_.3, f32[8]{0:T(128)} %refs_2_.2, f32[8]{0:T(128)} %refs_3_.1, ...), custom_call_target="tpu_custom_call" | custom-call | flops 1073741824 | bytes 8388608 | tf_op jit(solution)/shard_map/coarse/pallas_call | solution.py:304
  21.2 0.0 collective-permute-done.6.refs_2_
  21.2 0.0 collective-permute-done.7.refs_3_
  21.2 0.0 collective-permute-done.5.refs_1_
  21.2 0.0 collective-permute-done.4.refs_0_
  21.2 0.0 copy-done.1
  21.3 0.0 copy-done
  21.3 2.2 %unpack.1 = (f32[32,8,4096]{2,1,0:T(8,128)}, f32[3,8,8,4096]{3,2,1,0:T(8,128)}) custom-call(s32[3,5,8,128]{3,2,1,0:T(8,128)S(1)} %get-tuple-element.54.plan_ref, f32[8,8448]{1,0:T(8,128)S(1)} %collective-permute-done.4.refs_0_, f32[8,4352]{1,0:T(8,128)S(1)} %collective-permute-done.5.refs_1_, ...), custom_call_target="tpu_custom_call", output_to_operand_aliasing={{0}: (8, {})} | custom-call | flops 402653184 | bytes 5242880 | tf_op jit(solution)/shard_map/unpack/pallas_call | solution.py:415
  (1 shorter events, 0.0 us)
Async XLA Ops:
  0.6 20.6 %copy-start.1 = (s32[256]{0:T(256)S(1)}, s32[256]{0:T(256)}, u32[]{:S(2)}) copy-start(s32[256]{0:T(256)} %refs_1_.3) | copy-start | bytes 3076
  0.6 20.6 %copy-start = (s32[256]{0:T(256)S(1)}, s32[256]{0:T(256)}, u32[]{:S(2)}) copy-start(s32[256]{0:T(256)} %refs_0_.3) | copy-start | bytes 3076
  2.3 19.0 %collective-permute-start.4 = (f32[8,8448]{1,0:T(8,128)S(1)}, f32[8,8448]{1,0:T(8,128)S(1)}, u32[]{:S(2)}, u32[]{:S(2)}) collective-permute-start(f32[8,8448]{1,0:T(8,128)S(1)} %get-tuple-element.56), channel_id=1, source_target_pairs={{0,1},{2,3},{4,5},{6,7},{8,9},{10,11},{12,13},{14,15},{16,17},{18,... | collective-permute-start | bytes 811016 | tf_op jit(solution)/shard_map/ppermute | solution.py:34
  3.6 17.7 %collective-permute-start.5 = (f32[8,4352]{1,0:T(8,128)S(1)}, f32[8,4352]{1,0:T(8,128)S(1)}, u32[]{:S(2)}, u32[]{:S(2)}) collective-permute-start(f32[8,4352]{1,0:T(8,128)S(1)} %get-tuple-element.57), channel_id=1, source_target_pairs={{1,2},{3,4},{5,6},{7,8},{9,10},{11,12},{13,14},{15,16},{17,18},{19... | collective-permute-start | bytes 417800 | tf_op jit(solution)/shard_map/ppermute | solution.py:34
  8.1 13.1 %collective-permute-start.6 = (f32[8,4096]{1,0:T(8,128)S(1)}, f32[8,4096]{1,0:T(8,128)S(1)}, u32[]{:S(2)}, u32[]{:S(2)}) collective-permute-start(f32[8,4096]{1,0:T(8,128)S(1)} %get-tuple-element.58), channel_id=1, source_target_pairs={{0,2},{1,3},{4,6},{5,7},{8,10},{9,11},{12,14},{13,15},{16,18},{17,... | collective-permute-start | bytes 393224 | tf_op jit(solution)/shard_map/ppermute | solution.py:34
  8.2 13.0 %collective-permute-start.7 = (f32[8,4096]{1,0:T(8,128)S(1)}, f32[8,4096]{1,0:T(8,128)S(1)}, u32[]{:S(2)}, u32[]{:S(2)}) collective-permute-start(f32[8,4096]{1,0:T(8,128)S(1)} %get-tuple-element.59), channel_id=1, source_target_pairs={{2,4},{3,5},{6,8},{7,9},{10,12},{11,13},{14,16},{15,17},{18,20},{1... | collective-permute-start | bytes 393224 | tf_op jit(solution)/shard_map/ppermute | solution.py:34
where the time goes:
time: 23.6 us; the launch traced here: 23.4 us
  starting transfers between devices  13.2 us (56%)
  Pallas kernels  8.81 us (37%)
  between operations  1.39 us (6%)
    ppermute x4, starting transfers between devices, exchange(): lax.ppermute(part, AXES, pairs[way])  13.2 us
    pallas_call x1, Pallas kernels, coarse(): pl.pallas_call(coarse_kernel, out_shape=[pltpu.HBM(cons.shape, jnp.float3...  5.04 us
    pallas_call x1, Pallas kernels, unpack(): pl.pallas_call(unpack_kernel, out_shape=[pltpu.HBM(stepped.shape, jnp.flo...  2.16 us
    pallas_call x1, Pallas kernels, pack(): pl.pallas_call(functools.partial(pack_kernel, later), out_shape=[jax.Shap...  1.61 us
  transfers between devices with their start and end apart: 4, of which 0 were waited for; matrix products, arithmetic and copies ran while one was open for 0% of the time, Pallas kernels for 22%

commit v1 on v0

--- a/solution.py
+++ b/solution.py
@@ -14,8 +14,8 @@
 AXES = ("morton", "lane")
 CAP = 3
 HOLD = 4
-EVEN, ODD, WITHIN, ACROSS, HOME = range(5)
-ROOM = (2, 1, 1, 1)
+ODD, EVEN, ACROSS, WITHIN, HOME = range(5)
+ROOM = (2, 2, 1, 1)
 RIMS = (EVEN, ODD)
 PLACES = [(way, rank) for way in range(HOME) for rank in range(ROOM[way])]
 CHUNK = 8
@@ -26,7 +26,7 @@
     even = [(i, i + 1) for i in range(0, count - 1, 2)]
     across = [(i, i + 2) for i in range(count - 2) if i % 4 >= 2]
     within = [(i, i + 2) for i in range(count - 2) if i % 4 < 2]
-    return [pairs + [(b, a) for a, b in pairs] for pairs in (even, odd, within, across)]
+    return [pairs + [(b, a) for a, b in pairs] for pairs in (odd, even, across, within)]
 
 
 def exchange(parts):

time: 23.6 us -> 24.9 us (1.055)
  the two profiles are of different devices: /device:TPU:97 before, /device:TPU:1 now
where the time goes in v1:
time: 24.9 us; the launch traced here: 24.8 us
  starting transfers between devices  12.3 us (49%)
  Pallas kernels  8.81 us (35%)
  waiting for transfers between devices  2.32 us (9%)
  between operations  1.36 us (5%)
    ppermute x4, starting transfers between devices, exchange(): lax.ppermute(part, AXES, pairs[way])  12.3 us
    pallas_call x1, Pallas kernels, coarse(): pl.pallas_call(coarse_kernel, out_shape=[pltpu.HBM(cons.shape, jnp.float3...  5.03 us
    ppermute x4, waiting for transfers between devices, exchange(): lax.ppermute(part, AXES, pairs[way])  2.32 us
    pallas_call x1, Pallas kernels, unpack(): pl.pallas_call(unpack_kernel, out_shape=[pltpu.HBM(stepped.shape, jnp.flo...  2.17 us
    pallas_call x1, Pallas kernels, pack(): pl.pallas_call(functools.partial(pack_kernel, later), out_shape=[jax.Shap...  1.61 us
  transfers between devices with their start and end apart: 4, of which 1 were waited for; matrix products, arithmetic and copies ran while one was open for 0% of the time, Pallas kernels for 20%

profile of v1, /device:TPU:1, one launch (start us, length us, event | category | flops | bytes accessed | tf_op | source)
XLA Modules:
  0.0 24.8 jit_solution(10358955730885841614)
XLA Ops:
  0.6 0.0 copy-start.1
  0.6 0.0 copy-start
  0.7 1.6 %pack.2 = (f32[8,8448]{1,0:T(8,128)S(1)}, f32[8,8448]{1,0:T(8,128)S(1)}, f32[8,4096]{1,0:T(8,128)S(1)}, f32[8,4096]{1,0:T(8,128)S(1)}) custom-call(s32[256]{0:T(256)} %refs_0_.3, s32[256]{0:T(256)} %refs_1_.3, f32[32,8,4096]{2,1,0:T(8,128)} %refs_2_.3), custom_call_target="tpu_custom_call" | custom-call | bytes 1048576 | tf_op jit(solution)/shard_map/pack/pallas_call | solution.py:152
  2.3 6.1 %collective-permute-start.4 = (f32[8,8448]{1,0:T(8,128)S(1)}, f32[8,8448]{1,0:T(8,128)S(1)}, u32[]{:S(2)}, u32[]{:S(2)}) collective-permute-start(f32[8,8448]{1,0:T(8,128)S(1)} %get-tuple-element.56), channel_id=1, source_target_pairs={{1,2},{3,4},{5,6},{7,8},{9,10},{11,12},{13,14},{15,16},{17,18},{19... | collective-permute-start | bytes 811016 | tf_op jit(solution)/shard_map/ppermute | solution.py:34
  8.4 0.1 collective-permute-start.5
  8.5 3.4 %collective-permute-start.6 = (f32[8,4096]{1,0:T(8,128)S(1)}, f32[8,4096]{1,0:T(8,128)S(1)}, u32[]{:S(2)}, u32[]{:S(2)}) collective-permute-start(f32[8,4096]{1,0:T(8,128)S(1)} %get-tuple-element.58), channel_id=1, source_target_pairs={{2,4},{3,5},{6,8},{7,9},{10,12},{11,13},{14,16},{15,17},{18,20},{1... | collective-permute-start | bytes 393224 | tf_op jit(solution)/shard_map/ppermute | solution.py:34
  11.9 2.7 %collective-permute-start.7 = (f32[8,4096]{1,0:T(8,128)S(1)}, f32[8,4096]{1,0:T(8,128)S(1)}, u32[]{:S(2)}, u32[]{:S(2)}) collective-permute-start(f32[8,4096]{1,0:T(8,128)S(1)} %get-tuple-element.59), channel_id=1, source_target_pairs={{0,2},{1,3},{4,6},{5,7},{8,10},{9,11},{12,14},{13,15},{16,18},{17,... | collective-permute-start | bytes 393224 | tf_op jit(solution)/shard_map/ppermute | solution.py:34
  14.6 5.0 %coarse.1 = (f32[32,8,4096]{2,1,0:T(8,128)}, f32[4,8,256]{2,1,0:T(8,128)S(1)}, bf16[256,1024]{1,0:T(8,128)(2,1)S(1)}, f32[3,8,4096]{2,1,0:T(8,128)S(1)}, s32[3,6,8,128]{3,2,1,0:T(8,128)S(1)}, /*index=5*/s32[1]{0:T(128)}) custom-call(s32[256]{0:T(256)} %refs_0_.3, s32[256]{0:T(256)} %refs_1_.3, f32[8]{0:T(128)} %refs_2_.2, f32[8]{0:T(128)} %refs_3_.1, ...), custom_call_target="tpu_custom_call" | custom-call | flops 1073741824 | bytes 8388608 | tf_op jit(solution)/shard_map/coarse/pallas_call | solution.py:304
  20.3 0.0 collective-permute-done.6.refs_2_
  20.3 2.3 %collective-permute-done.7.refs_3_ = f32[8,4096]{1,0:T(8,128)S(1)} collective-permute-done((f32[8,4096]{1,0:T(8,128)S(1)}, f32[8,4096]{1,0:T(8,128)S(1)}, u32[]{:S(2)}, u32[]{:S(2)}) %collective-permute-start.7) | collective-permute-done | bytes 131104 | tf_op jit(solution)/shard_map/ppermute | solution.py:34
  22.6 0.0 collective-permute-done.4.refs_0_
  22.6 0.0 collective-permute-done.5.refs_1_
  22.6 0.0 copy-done.1
  22.6 0.0 copy-done
  22.7 2.2 %unpack.1 = (f32[32,8,4096]{2,1,0:T(8,128)}, f32[3,8,8,4096]{3,2,1,0:T(8,128)}) custom-call(s32[3,6,8,128]{3,2,1,0:T(8,128)S(1)} %get-tuple-element.54.plan_ref, f32[8,8448]{1,0:T(8,128)S(1)} %collective-permute-done.4.refs_0_, f32[8,8448]{1,0:T(8,128)S(1)} %collective-permute-done.5.refs_1_, ...), custom_call_target="tpu_custom_call", output_to_operand_aliasing={{0}: (8, {})} | custom-call | flops 402653184 | bytes 5242880 | tf_op jit(solution)/shard_map/unpack/pallas_call | solution.py:415
  (1 shorter events, 0.0 us)
Async XLA Ops:
  0.6 22.0 %copy-start.1 = (s32[256]{0:T(256)S(1)}, s32[256]{0:T(256)}, u32[]{:S(2)}) copy-start(s32[256]{0:T(256)} %refs_1_.3) | copy-start | bytes 3076
  0.6 22.0 %copy-start = (s32[256]{0:T(256)S(1)}, s32[256]{0:T(256)}, u32[]{:S(2)}) copy-start(s32[256]{0:T(256)} %refs_0_.3) | copy-start | bytes 3076
  2.3 20.3 %collective-permute-start.4 = (f32[8,8448]{1,0:T(8,128)S(1)}, f32[8,8448]{1,0:T(8,128)S(1)}, u32[]{:S(2)}, u32[]{:S(2)}) collective-permute-start(f32[8,8448]{1,0:T(8,128)S(1)} %get-tuple-element.56), channel_id=1, source_target_pairs={{1,2},{3,4},{5,6},{7,8},{9,10},{11,12},{13,14},{15,16},{17,18},{19... | collective-permute-start | bytes 811016 | tf_op jit(solution)/shard_map/ppermute | solution.py:34
  8.4 14.2 %collective-permute-start.5 = (f32[8,8448]{1,0:T(8,128)S(1)}, f32[8,8448]{1,0:T(8,128)S(1)}, u32[]{:S(2)}, u32[]{:S(2)}) collective-permute-start(f32[8,8448]{1,0:T(8,128)S(1)} %get-tuple-element.57), channel_id=1, source_target_pairs={{0,1},{2,3},{4,5},{6,7},{8,9},{10,11},{12,13},{14,15},{16,17},{18,... | collective-permute-start | bytes 811016 | tf_op jit(solution)/shard_map/ppermute | solution.py:34
  8.5 11.8 %collective-permute-start.6 = (f32[8,4096]{1,0:T(8,128)S(1)}, f32[8,4096]{1,0:T(8,128)S(1)}, u32[]{:S(2)}, u32[]{:S(2)}) collective-permute-start(f32[8,4096]{1,0:T(8,128)S(1)} %get-tuple-element.58), channel_id=1, source_target_pairs={{2,4},{3,5},{6,8},{7,9},{10,12},{11,13},{14,16},{15,17},{18,20},{1... | collective-permute-start | bytes 393224 | tf_op jit(solution)/shard_map/ppermute | solution.py:34
  11.9 10.7 %collective-permute-start.7 = (f32[8,4096]{1,0:T(8,128)S(1)}, f32[8,4096]{1,0:T(8,128)S(1)}, u32[]{:S(2)}, u32[]{:S(2)}) collective-permute-start(f32[8,4096]{1,0:T(8,128)S(1)} %get-tuple-element.59), channel_id=1, source_target_pairs={{0,2},{1,3},{4,6},{5,7},{8,10},{9,11},{12,14},{13,15},{16,18},{17,... | collective-permute-start | bytes 393224 | tf_op jit(solution)/shard_map/ppermute | solution.py:34

commit v2 on v0

--- a/solution.py
+++ b/solution.py
@@ -207,8 +207,8 @@
 
 
 def coarse_kernel(*refs):
-    scalars, (flagged_hbm, owner_hbm, cons_hbm, out_ref, edge_ref, table_ref, home_ref, plan_ref, left_hbm), refs = refs[:4], refs[4:13], refs[13:]
-    copies, (left_ref, flagged_row, owner_row, cons_ref, next_ref, sem, few) = refs[:4], refs[4:]
+    scalars, (flagged_hbm, owner_hbm, cons_hbm, out_ref, edge_ref, table_ref, home_ref, plan_ref, left_ref), refs = refs[:4], refs[4:13], refs[13:]
+    copies, (flagged_row, owner_row, cons_ref, next_ref, sem, few) = refs[:4], refs[4:]
     flagged_ref, owner_ref, diff_ref, cour_ref = copies
     own, fields, _ = cons_ref.shape
     turns = own // CHUNK
@@ -230,8 +230,6 @@
     for copy in few_copies:
         copy.wait()
     left_ref[0] = rounds_left(flagged_row[...], owner_row[...], own)
-    left_copy = pltpu.make_async_copy(left_ref, left_hbm, few.at[len(few_copies)])
-    left_copy.start()
     diffuse = by_field(diff_ref, fields)
     courant = by_field(cour_ref, fields)
     centre = 1.0 - 6.0 * diffuse - courant
@@ -294,7 +292,6 @@
     edge_ref[1] = next_ref[own - 1, :, pl.ds(CELLS - PLANE, PLANE)]
     for turn in range(turns):
         store(turn).wait()
-    left_copy.wait()
 
 
 def coarse(flagged, owner, diffusivity, courant, cons):
@@ -309,13 +306,12 @@
             jax.ShapeDtypeStruct((PLANE, 4 * PLANE), jnp.bfloat16),
             jax.ShapeDtypeStruct((CAP, fields, cells), jnp.float32),
             jax.ShapeDtypeStruct((CAP, len(PLACES), fields, 128), jnp.int32),
-            pltpu.HBM((1,), jnp.int32),
+            pltpu.SMEM((1,), jnp.int32),
         ],
         in_specs=[hbm] * 7,
-        out_specs=[hbm, vmem, vmem, vmem, vmem, hbm],
+        out_specs=[hbm, vmem, vmem, vmem, vmem, pl.BlockSpec(memory_space=pltpu.SMEM)],
         scratch_shapes=[
             *(pltpu.SMEM(value.shape, value.dtype) for value in (flagged, owner, diffusivity, courant)),
-            pltpu.SMEM((1,), jnp.int32),
             pltpu.VMEM((1, flagged.shape[0]), jnp.int32),
             pltpu.VMEM((1, owner.shape[0]), jnp.int32),
             pltpu.VMEM(cons.shape, jnp.float32),
@@ -433,7 +429,7 @@
     own = cons_old.shape[0]
     arrived = exchange(pack(flagged, new_owner, cons_old))
     stepped, edges, table, home, plan, left = coarse(flagged, new_owner, diffusivity, courant, cons_old)
-    left = jnp.maximum(left.reshape(()), 0)
+    left = left.reshape(())
 
     def later(carry):
         turn, home = carry

time: 23.6 us -> 23.4 us (level)
  the two profiles are of different devices: /device:TPU:97 before, /device:TPU:96 now
where the time goes in v2:
time: 23.4 us; the launch traced here: 22.9 us
  starting transfers between devices  12.8 us (55%)
  Pallas kernels  9.21 us (39%)
  between operations  0.71 us (3%)
    ppermute x4, starting transfers between devices, exchange(): lax.ppermute(part, AXES, pairs[way])  12.8 us
    pallas_call x1, Pallas kernels, coarse(): pl.pallas_call(coarse_kernel, out_shape=[pltpu.HBM(cons.shape, jnp.float3...  5.04 us
    pallas_call x1, Pallas kernels, unpack(): pl.pallas_call(unpack_kernel, out_shape=[pltpu.HBM(stepped.shape, jnp.flo...  2.16 us
    pallas_call x1, Pallas kernels, pack(): pl.pallas_call(functools.partial(pack_kernel, later), out_shape=[jax.Shap...  2.01 us
  transfers between devices with their start and end apart: 4, of which 1 were waited for; matrix products, arithmetic and copies ran while one was open for 0% of the time, Pallas kernels for 22%

profile of v2, /device:TPU:96, one launch (start us, length us, event | category | flops | bytes accessed | tf_op | source)
XLA Modules:
  0.0 22.9 jit_solution(17776022707874077916)
XLA Ops:
  0.6 0.0 copy-start.1
  0.6 0.0 copy-start
  0.7 2.0 %pack.2 = (f32[8,8448]{1,0:T(8,128)S(1)}, f32[8,4352]{1,0:T(8,128)S(1)}, f32[8,4096]{1,0:T(8,128)S(1)}, f32[8,4096]{1,0:T(8,128)S(1)}) custom-call(s32[256]{0:T(256)} %refs_0_.3, s32[256]{0:T(256)} %refs_1_.3, f32[32,8,4096]{2,1,0:T(8,128)} %refs_2_.3), custom_call_target="tpu_custom_call" | custom-call | bytes 1048576 | tf_op jit(solution)/shard_map/pack/pallas_call | solution.py:152
  2.7 1.2 %collective-permute-start.4 = (f32[8,8448]{1,0:T(8,128)S(1)}, f32[8,8448]{1,0:T(8,128)S(1)}, u32[]{:S(2)}, u32[]{:S(2)}) collective-permute-start(f32[8,8448]{1,0:T(8,128)S(1)} %get-tuple-element.56), channel_id=1, source_target_pairs={{0,1},{2,3},{4,5},{6,7},{8,9},{10,11},{12,13},{14,15},{16,17},{18,... | collective-permute-start | bytes 811016 | tf_op jit(solution)/shard_map/ppermute | solution.py:34
  3.8 5.9 %collective-permute-start.5 = (f32[8,4352]{1,0:T(8,128)S(1)}, f32[8,4352]{1,0:T(8,128)S(1)}, u32[]{:S(2)}, u32[]{:S(2)}) collective-permute-start(f32[8,4352]{1,0:T(8,128)S(1)} %get-tuple-element.57), channel_id=1, source_target_pairs={{1,2},{3,4},{5,6},{7,8},{9,10},{11,12},{13,14},{15,16},{17,18},{19... | collective-permute-start | bytes 417800 | tf_op jit(solution)/shard_map/ppermute | solution.py:34
  9.7 0.1 collective-permute-start.6
  9.8 5.7 %collective-permute-start.7 = (f32[8,4096]{1,0:T(8,128)S(1)}, f32[8,4096]{1,0:T(8,128)S(1)}, u32[]{:S(2)}, u32[]{:S(2)}) collective-permute-start(f32[8,4096]{1,0:T(8,128)S(1)} %get-tuple-element.59), channel_id=1, source_target_pairs={{2,4},{3,5},{6,8},{7,9},{10,12},{11,13},{14,16},{15,17},{18,20},{1... | collective-permute-start | bytes 393224 | tf_op jit(solution)/shard_map/ppermute | solution.py:34
  15.5 5.0 %coarse.1 = (f32[32,8,4096]{2,1,0:T(8,128)}, f32[4,8,256]{2,1,0:T(8,128)S(1)}, bf16[256,1024]{1,0:T(8,128)(2,1)S(1)}, f32[3,8,4096]{2,1,0:T(8,128)S(1)}, s32[3,5,8,128]{3,2,1,0:T(8,128)S(1)}, /*index=5*/s32[1]{0:T(128)S(4)}) custom-call(s32[256]{0:T(256)} %refs_0_.3, s32[256]{0:T(256)} %refs_1_.3, f32[8]{0:T(128)} %refs_2_.2, f32[8]{0:T(128)} %refs_3_.1, ...), custom_call_target="tpu_custom_call" | custom-call | flops 1073741824 | bytes 8388608 | tf_op jit(solution)/shard_map/coarse/pallas_call | solution.py:301
  20.6 0.0 collective-permute-done.6.refs_2_
  20.6 0.1 collective-permute-done.7.refs_3_
  20.7 0.0 collective-permute-done.5.refs_1_
  20.7 0.0 collective-permute-done.4.refs_0_
  20.7 0.0 copy-done.1
  20.7 0.0 copy-done
  20.7 2.2 %unpack.1 = (f32[32,8,4096]{2,1,0:T(8,128)}, f32[3,8,8,4096]{3,2,1,0:T(8,128)}) custom-call(s32[3,5,8,128]{3,2,1,0:T(8,128)S(1)} %get-tuple-element.54.plan_ref, f32[8,8448]{1,0:T(8,128)S(1)} %collective-permute-done.4.refs_0_, f32[8,4352]{1,0:T(8,128)S(1)} %collective-permute-done.5.refs_1_, ...), custom_call_target="tpu_custom_call", output_to_operand_aliasing={{0}: (8, {})} | custom-call | flops 402653184 | bytes 5242880 | tf_op jit(solution)/shard_map/unpack/pallas_call | solution.py:411
  (1 shorter events, 0.0 us)
Async XLA Ops:
  0.6 20.1 %copy-start.1 = (s32[256]{0:T(256)S(1)}, s32[256]{0:T(256)}, u32[]{:S(2)}) copy-start(s32[256]{0:T(256)} %refs_1_.3) | copy-start | bytes 3076
  0.6 20.1 %copy-start = (s32[256]{0:T(256)S(1)}, s32[256]{0:T(256)}, u32[]{:S(2)}) copy-start(s32[256]{0:T(256)} %refs_0_.3) | copy-start | bytes 3076
  2.7 18.0 %collective-permute-start.4 = (f32[8,8448]{1,0:T(8,128)S(1)}, f32[8,8448]{1,0:T(8,128)S(1)}, u32[]{:S(2)}, u32[]{:S(2)}) collective-permute-start(f32[8,8448]{1,0:T(8,128)S(1)} %get-tuple-element.56), channel_id=1, source_target_pairs={{0,1},{2,3},{4,5},{6,7},{8,9},{10,11},{12,13},{14,15},{16,17},{18,... | collective-permute-start | bytes 811016 | tf_op jit(solution)/shard_map/ppermute | solution.py:34
  3.8 16.8 %collective-permute-start.5 = (f32[8,4352]{1,0:T(8,128)S(1)}, f32[8,4352]{1,0:T(8,128)S(1)}, u32[]{:S(2)}, u32[]{:S(2)}) collective-permute-start(f32[8,4352]{1,0:T(8,128)S(1)} %get-tuple-element.57), channel_id=1, source_target_pairs={{1,2},{3,4},{5,6},{7,8},{9,10},{11,12},{13,14},{15,16},{17,18},{19... | collective-permute-start | bytes 417800 | tf_op jit(solution)/shard_map/ppermute | solution.py:34
  9.7 10.8 %collective-permute-start.6 = (f32[8,4096]{1,0:T(8,128)S(1)}, f32[8,4096]{1,0:T(8,128)S(1)}, u32[]{:S(2)}, u32[]{:S(2)}) collective-permute-start(f32[8,4096]{1,0:T(8,128)S(1)} %get-tuple-element.58), channel_id=1, source_target_pairs={{0,2},{1,3},{4,6},{5,7},{8,10},{9,11},{12,14},{13,15},{16,18},{17,... | collective-permute-start | bytes 393224 | tf_op jit(solution)/shard_map/ppermute | solution.py:34
  9.8 10.9 %collective-permute-start.7 = (f32[8,4096]{1,0:T(8,128)S(1)}, f32[8,4096]{1,0:T(8,128)S(1)}, u32[]{:S(2)}, u32[]{:S(2)}) collective-permute-start(f32[8,4096]{1,0:T(8,128)S(1)} %get-tuple-element.59), channel_id=1, source_target_pairs={{2,4},{3,5},{6,8},{7,9},{10,12},{11,13},{14,16},{15,17},{18,20},{1... | collective-permute-start | bytes 393224 | tf_op jit(solution)/shard_map/ppermute | solution.py:34

commit v3 on v2

--- a/solution.py
+++ b/solution.py
@@ -18,6 +18,7 @@
 ROOM = (2, 1, 1, 1)
 RIMS = (EVEN, ODD)
 PLACES = [(way, rank) for way in range(HOME) for rank in range(ROOM[way])]
+KEPT, EMPTY = len(PLACES), len(PLACES) + 1
 CHUNK = 8
 
 
@@ -207,8 +208,8 @@
 
 
 def coarse_kernel(*refs):
-    scalars, (flagged_hbm, owner_hbm, cons_hbm, out_ref, edge_ref, table_ref, home_ref, plan_ref, left_ref), refs = refs[:4], refs[4:13], refs[13:]
-    copies, (flagged_row, owner_row, cons_ref, next_ref, sem, few) = refs[:4], refs[4:]
+    scalars, (flagged_hbm, owner_hbm, cons_hbm, out_ref, children_ref, edge_ref, table_ref, home_ref, plan_ref, left_ref), refs = refs[:4], refs[4:14], refs[14:]
+    copies, (flagged_row, owner_row, cons_ref, next_ref, zero_ref, sem, few) = refs[:4], refs[4:]
     flagged_ref, owner_ref, diff_ref, cour_ref = copies
     own, fields, _ = cons_ref.shape
     turns = own // CHUNK
@@ -220,6 +221,11 @@
     def load(i):
         span = pl.ds(pl.multiple_of(i * part, part), part)
         return pltpu.make_async_copy(cons_hbm.at[span], cons_ref.at[span], sem.at[turns + i])
+
+    zero_ref[...] = jnp.zeros(zero_ref.shape, jnp.float32)
+
+    def put(s):
+        return pltpu.make_async_copy(zero_ref, children_ref.at[s], few.at[len(copies) + 2 + s])
 
     few_copies = [pltpu.make_async_copy(*pair, few.at[i]) for i, pair in enumerate(zip((*scalars, flagged_hbm, owner_hbm), (*copies, flagged_row, owner_row)))]
     for copy in few_copies:
@@ -230,6 +236,14 @@
     for copy in few_copies:
         copy.wait()
     left_ref[0] = rounds_left(flagged_row[...], owner_row[...], own)
+    found = arrivals(flagged_ref, owner_ref, own, me)
+    for s, (mine, _, way, rank) in enumerate(found):
+        place = jnp.where(mine, KEPT, EMPTY)
+        for i, (c, r) in enumerate(PLACES):
+            place = jnp.where(mine & (way == c) & (rank == r), i, place)
+        plan_ref[s] = place
+        pl.when(jnp.logical_not(mine))(put(s).start)
+
     diffuse = by_field(diff_ref, fields)
     courant = by_field(cour_ref, fields)
     centre = 1.0 - 6.0 * diffuse - courant
@@ -271,12 +285,6 @@
     for q in range(4):
         table_ref[:, pl.ds(q * PLANE, PLANE)] = refine_quarter(q)
 
-    found = arrivals(flagged_ref, owner_ref, own, me)
-    for s, (mine, _, way, rank) in enumerate(found):
-        for i, (c, r) in enumerate(PLACES):
-            comes = mine & (way == c) & (rank == r)
-            plan_ref[s, i] = jnp.full(plan_ref.shape[2:], comes.astype(jnp.int32))
-
     for s, (mine, block, way, _) in enumerate(found):
         stays = mine & (way == HOME)
 
@@ -292,32 +300,37 @@
     edge_ref[1] = next_ref[own - 1, :, pl.ds(CELLS - PLANE, PLANE)]
     for turn in range(turns):
         store(turn).wait()
+    for s, (mine, _, _, _) in enumerate(found):
+        pl.when(jnp.logical_not(mine))(put(s).wait)
 
 
 def coarse(flagged, owner, diffusivity, courant, cons):
     own, fields, cells = cons.shape
+    smem = pl.BlockSpec(memory_space=pltpu.SMEM)
     vmem = pl.BlockSpec(memory_space=pltpu.VMEM)
     hbm = pl.BlockSpec(memory_space=pltpu.HBM)
     return pl.pallas_call(
         coarse_kernel,
         out_shape=[
             pltpu.HBM(cons.shape, jnp.float32),
+            pltpu.HBM((CAP, 8, fields, cells), jnp.float32),
             jax.ShapeDtypeStruct((4, fields, PLANE), jnp.float32),
             jax.ShapeDtypeStruct((PLANE, 4 * PLANE), jnp.bfloat16),
             jax.ShapeDtypeStruct((CAP, fields, cells), jnp.float32),
-            jax.ShapeDtypeStruct((CAP, len(PLACES), fields, 128), jnp.int32),
+            pltpu.SMEM((CAP,), jnp.int32),
             pltpu.SMEM((1,), jnp.int32),
         ],
         in_specs=[hbm] * 7,
-        out_specs=[hbm, vmem, vmem, vmem, vmem, pl.BlockSpec(memory_space=pltpu.SMEM)],
+        out_specs=[hbm, hbm, vmem, vmem, vmem, smem, smem],
         scratch_shapes=[
             *(pltpu.SMEM(value.shape, value.dtype) for value in (flagged, owner, diffusivity, courant)),
             pltpu.VMEM((1, flagged.shape[0]), jnp.int32),
             pltpu.VMEM((1, owner.shape[0]), jnp.int32),
             pltpu.VMEM(cons.shape, jnp.float32),
             pltpu.VMEM(cons.shape, jnp.float32),
+            pltpu.VMEM((8, fields, cells), jnp.float32),
             pltpu.SemaphoreType.DMA((3 * (own // CHUNK),)),
-            pltpu.SemaphoreType.DMA((7,)),
+            pltpu.SemaphoreType.DMA((6 + CAP,)),
         ],
         compiler_params=pltpu.CompilerParams(vmem_limit_bytes=20 << 20),
         cost_estimate=pl.CostEstimate(flops=2 * 2 * own * EDGE * fields * PLANE * PLANE, bytes_accessed=8 << 20, transcendentals=0),
@@ -355,7 +368,7 @@
 
 
 def unpack_kernel(plan_ref, *refs):
-    parts, (home_ref, edge_ref, table_ref, _, coarse_ref, children_ref, child_ref, rim_ref, sem) = refs[:HOME], refs[HOME:]
+    parts, (home_ref, edge_ref, table_ref, _, _, coarse_ref, children_ref, parent_ref, child_ref, rim_ref, sem) = refs[:HOME], refs[HOME:]
     own, fields, _ = coarse_ref.shape
     me = lax.axis_index(AXES)
     rims = [parts[way][:, pl.ds(ROOM[way] * CELLS, PLANE)] for way in RIMS]
@@ -363,47 +376,45 @@
     rim_ref[0] = edge_ref[0] + edge_ref[3] * jnp.where(odd, rims[0], rims[1])
     rim_ref[1] = edge_ref[1] + edge_ref[2] * jnp.where(odd, rims[1], rims[0])
     spots = (coarse_ref.at[0, :, pl.ds(0, PLANE)], coarse_ref.at[own - 1, :, pl.ds(CELLS - PLANE, PLANE)])
-    ends = [pltpu.make_async_copy(rim_ref.at[c], spots[c], sem.at[CAP * 8 + c]) for c in range(2)]
+    ends = [pltpu.make_async_copy(rim_ref.at[c], spots[c], sem.at[CAP + c]) for c in range(2)]
     for copy in ends:
         copy.start()
 
     def store(s, child):
-        return pltpu.make_async_copy(child_ref.at[s, child], children_ref.at[s, child], sem.at[s * 8 + child])
+        return pltpu.make_async_copy(child_ref.at[s, child], children_ref.at[s, child], sem.at[s])
 
     @pl.loop(0, CAP)
     def _(s):
-        comes = [plan_ref[s, i] != 0 for i in range(len(PLACES))]
-        planes = []
-        for x in range(EDGE):
-            halves = []
-            for column in range(x * PLANE, (x + 1) * PLANE, 128):
-                value = home_ref[s, :, pl.ds(column, 128)]
-                for i, (c, r) in enumerate(PLACES):
-                    value = jnp.where(comes[i], parts[c][:, pl.ds(r * CELLS + column, 128)], value)
-                halves.append(value)
-            planes.append(jnp.concatenate(halves, 1))
-        parent = split(jnp.concatenate(planes, 0))
-        for q in range(4):
-            fine = dot_split(parent, table_ref[:, pl.ds(q * PLANE, PLANE)])
-            rows = [fine[x * fields : (x + 1) * fields] for x in range(EDGE)]
-            for x in range(EDGE):
-                low, high = max(x - 1, 0), min(x + 1, EDGE - 1)
-                slope = (rows[high] - rows[low]) * (0.25 / (high - low))
-                half, place = divmod(2 * x, EDGE)
-                child_ref[s, half * 4 + q, :, pl.ds(place * PLANE, PLANE)] = rows[x] - slope
-                child_ref[s, half * 4 + q, :, pl.ds((place + 1) * PLANE, PLANE)] = rows[x] + slope
-            for half in range(2):
-                store(s, half * 4 + q).start()
-
-    @pl.loop(0, CAP * 8)
-    def _(i):
-        store(i >> 3, i & 7).wait()
+        for i, (c, r) in enumerate([*PLACES, (None, None)]):
+
+            @pl.when(plan_ref[s] == i)
+            def _():
+                parent_ref[...] = home_ref[s] if c is None else parts[c][:, pl.ds(r * CELLS, CELLS)]
+
+        @pl.when(plan_ref[s] != EMPTY)
+        def _():
+            planes = [parent_ref[:, pl.ds(x * PLANE, PLANE)] for x in range(EDGE)]
+            parent = split(jnp.concatenate(planes, 0))
+            for q in range(4):
+                fine = dot_split(parent, table_ref[:, pl.ds(q * PLANE, PLANE)])
+                rows = [fine[x * fields : (x + 1) * fields] for x in range(EDGE)]
+                for x in range(EDGE):
+                    low, high = max(x - 1, 0), min(x + 1, EDGE - 1)
+                    slope = (rows[high] - rows[low]) * (0.25 / (high - low))
+                    half, place = divmod(2 * x, EDGE)
+                    child_ref[s, half * 4 + q, :, pl.ds(place * PLANE, PLANE)] = rows[x] - slope
+                    child_ref[s, half * 4 + q, :, pl.ds((place + 1) * PLANE, PLANE)] = rows[x] + slope
+                for half in range(2):
+                    store(s, half * 4 + q).start()
+
+    for s in range(CAP):
+        pl.when(plan_ref[s] != EMPTY)(pltpu.make_async_copy(child_ref.at[s], children_ref.at[s], sem.at[s]).wait)
 
     for copy in ends:
         copy.wait()
 
 
-def unpack(plan, parts, home, edges, table, stepped):
+def unpack(plan, parts, home, edges, table, stepped, children):
     fields = stepped.shape[1]
     vmem = pl.BlockSpec(memory_space=pltpu.VMEM)
     hbm = pl.BlockSpec(memory_space=pltpu.HBM)
@@ -411,24 +422,25 @@
     return pl.pallas_call(
         unpack_kernel,
         out_shape=[pltpu.HBM(stepped.shape, jnp.float32), family],
-        in_specs=[vmem] * (HOME + 4) + [hbm],
+        in_specs=[pl.BlockSpec(memory_space=pltpu.SMEM)] + [vmem] * (HOME + 3) + [hbm, hbm],
         out_specs=[hbm, hbm],
         scratch_shapes=[
+            pltpu.VMEM((fields, CELLS), jnp.float32),
             pltpu.VMEM(family.shape, jnp.float32),
             pltpu.VMEM((2, fields, PLANE), jnp.float32),
-            pltpu.SemaphoreType.DMA((CAP * 8 + 2,)),
+            pltpu.SemaphoreType.DMA((CAP + 2,)),
         ],
-        input_output_aliases={HOME + 4: 0},
+        input_output_aliases={HOME + 4: 0, HOME + 5: 1},
         compiler_params=pltpu.CompilerParams(vmem_limit_bytes=24 << 20),
         cost_estimate=pl.CostEstimate(flops=2 * 2 * CAP * EDGE * fields * PLANE * 4 * PLANE, bytes_accessed=5 << 20, transcendentals=0),
         name="unpack",
-    )(plan, *parts, home, edges, table, stepped)
+    )(plan, *parts, home, edges, table, stepped, children)
 
 
 def shards(cons_old, flagged, new_owner, diffusivity, courant):
     own = cons_old.shape[0]
     arrived = exchange(pack(flagged, new_owner, cons_old))
-    stepped, edges, table, home, plan, left = coarse(flagged, new_owner, diffusivity, courant, cons_old)
+    stepped, children, edges, table, home, plan, left = coarse(flagged, new_owner, diffusivity, courant, cons_old)
     left = left.reshape(())
 
     def later(carry):
@@ -439,7 +451,7 @@
 
     home, arrived = lax.optimization_barrier((home, arrived))
     _, home = lax.while_loop(lambda carry: carry[0] < left, later, (jnp.int32(0), home))
-    return tuple(unpack(plan, arrived, home, edges, table, stepped))
+    return tuple(unpack(plan, arrived, home, edges, table, stepped, children))
 
 
 def solution(mesh):

time: 23.4 us -> 23.4 us (level); the launches traced: 22.9 us -> 23.2 us
  Pallas kernels: 9.21 us -> 8.77 us
  waiting for transfers between devices: 0.13 us -> 0.55 us
  starting transfers between devices: 12.8 us -> 13.2 us
    ppermute x4, waiting for transfers between devices: 0.13 us -> 0.55 us  [exchange(): lax.ppermute(part, AXES, pairs[way])]
    pallas_call x1, Pallas kernels: 2.01 us -> 1.61 us  [pack(): pl.pallas_call(functools.partial(pack_kernel, later), out_shape=[jax.Shap...]
    ppermute x4, starting transfers between devices: 12.8 us -> 13.2 us  [exchange(): lax.ppermute(part, AXES, pairs[way])]
where the time goes in v3:
time: 23.4 us; the launch traced here: 23.2 us
  starting transfers between devices  13.2 us (56%)
  Pallas kernels  8.77 us (37%)
  between operations  0.71 us (3%)
  waiting for transfers between devices  0.55 us (2%)
    ppermute x4, starting transfers between devices, exchange(): lax.ppermute(part, AXES, pairs[way])  13.2 us
    pallas_call x1, Pallas kernels, coarse(): pl.pallas_call(coarse_kernel, out_shape=[pltpu.HBM(cons.shape, jnp.float3...  5.05 us
    pallas_call x1, Pallas kernels, unpack(): pl.pallas_call(unpack_kernel, out_shape=[pltpu.HBM(stepped.shape, jnp.flo...  2.1 us
    pallas_call x1, Pallas kernels, pack(): pl.pallas_call(functools.partial(pack_kernel, later), out_shape=[jax.Shap...  1.61 us
    ppermute x4, waiting for transfers between devices, exchange(): lax.ppermute(part, AXES, pairs[way])  0.55 us
  transfers between devices with their start and end apart: 4, of which 1 were waited for; matrix products, arithmetic and copies ran while one was open for 0% of the time, Pallas kernels for 22%

profile of v3, /device:TPU:96, one launch (start us, length us, event | category | flops | bytes accessed | tf_op | source)
XLA Modules:
  0.0 23.2 jit_solution(8981401539714693969)
XLA Ops:
  0.6 0.0 copy-start.1
  0.6 0.0 copy-start
  0.7 1.6 %pack.2 = (f32[8,8448]{1,0:T(8,128)S(1)}, f32[8,4352]{1,0:T(8,128)S(1)}, f32[8,4096]{1,0:T(8,128)S(1)}, f32[8,4096]{1,0:T(8,128)S(1)}) custom-call(s32[256]{0:T(256)} %refs_0_.3, s32[256]{0:T(256)} %refs_1_.3, f32[32,8,4096]{2,1,0:T(8,128)} %refs_2_.3), custom_call_target="tpu_custom_call" | custom-call | bytes 1048576 | tf_op jit(solution)/shard_map/pack/pallas_call | solution.py:153
  2.3 1.9 %collective-permute-start.4 = (f32[8,8448]{1,0:T(8,128)S(1)}, f32[8,8448]{1,0:T(8,128)S(1)}, u32[]{:S(2)}, u32[]{:S(2)}) collective-permute-start(f32[8,8448]{1,0:T(8,128)S(1)} %get-tuple-element.57), channel_id=1, source_target_pairs={{0,1},{2,3},{4,5},{6,7},{8,9},{10,11},{12,13},{14,15},{16,17},{18,... | collective-permute-start | bytes 811016 | tf_op jit(solution)/shard_map/ppermute | solution.py:35
  4.2 5.1 %collective-permute-start.5 = (f32[8,4352]{1,0:T(8,128)S(1)}, f32[8,4352]{1,0:T(8,128)S(1)}, u32[]{:S(2)}, u32[]{:S(2)}) collective-permute-start(f32[8,4352]{1,0:T(8,128)S(1)} %get-tuple-element.58), channel_id=1, source_target_pairs={{1,2},{3,4},{5,6},{7,8},{9,10},{11,12},{13,14},{15,16},{17,18},{19... | collective-permute-start | bytes 417800 | tf_op jit(solution)/shard_map/ppermute | solution.py:35
  9.3 0.1 collective-permute-start.6
  9.4 6.1 %collective-permute-start.7 = (f32[8,4096]{1,0:T(8,128)S(1)}, f32[8,4096]{1,0:T(8,128)S(1)}, u32[]{:S(2)}, u32[]{:S(2)}) collective-permute-start(f32[8,4096]{1,0:T(8,128)S(1)} %get-tuple-element.60), channel_id=1, source_target_pairs={{2,4},{3,5},{6,8},{7,9},{10,12},{11,13},{14,16},{15,17},{18,20},{1... | collective-permute-start | bytes 393224 | tf_op jit(solution)/shard_map/ppermute | solution.py:35
  15.5 5.1 %coarse.1 = (f32[32,8,4096]{2,1,0:T(8,128)}, f32[3,8,8,4096]{3,2,1,0:T(8,128)}, f32[4,8,256]{2,1,0:T(8,128)S(1)}, bf16[256,1024]{1,0:T(8,128)(2,1)S(1)}, f32[3,8...) custom-call(s32[256]{0:T(256)} %refs_0_.3, s32[256]{0:T(256)} %refs_1_.3, f32[8]{0:T(128)} %refs_2_.2, f32[8]{0:T(128)} %refs_3_.1, ...), custom_call_target="tpu_custom_call" | custom-call | flops 1073741824 | bytes 8388608 | tf_op jit(solution)/shard_map/coarse/pallas_call | solution.py:312
  20.5 0.0 collective-permute-done.6.refs_2_
  20.6 0.5 %collective-permute-done.7.refs_3_ = f32[8,4096]{1,0:T(8,128)S(1)} collective-permute-done((f32[8,4096]{1,0:T(8,128)S(1)}, f32[8,4096]{1,0:T(8,128)S(1)}, u32[]{:S(2)}, u32[]{:S(2)}) %collective-permute-start.7) | collective-permute-done | bytes 131104 | tf_op jit(solution)/shard_map/ppermute | solution.py:35
  21.1 0.0 collective-permute-done.5.refs_1_
  21.1 0.0 collective-permute-done.4.refs_0_
  21.1 0.0 copy-done.1
  21.1 0.0 copy-done
  21.1 2.1 %unpack.1 = (f32[32,8,4096]{2,1,0:T(8,128)}, f32[3,8,8,4096]{3,2,1,0:T(8,128)}) custom-call(s32[3]{0:T(128)S(4)} %get-tuple-element.55.plan_ref, f32[8,8448]{1,0:T(8,128)S(1)} %collective-permute-done.4.refs_0_, f32[8,4352]{1,0:T(8,128)S(1)} %collective-permute-done.5.refs_1_, ...), custom_call_target="tpu_custom_call", output_to_operand_aliasing={{0}: (8, {}), {1}: (9, {})} | custom-call | flops 402653184 | bytes 5242880 | tf_op jit(solution)/shard_map/unpack/pallas_call | solution.py:422
  (1 shorter events, 0.0 us)
Async XLA Ops:
  0.6 20.5 %copy-start.1 = (s32[256]{0:T(256)S(1)}, s32[256]{0:T(256)}, u32[]{:S(2)}) copy-start(s32[256]{0:T(256)} %refs_1_.3) | copy-start | bytes 3076
  0.6 20.5 %copy-start = (s32[256]{0:T(256)S(1)}, s32[256]{0:T(256)}, u32[]{:S(2)}) copy-start(s32[256]{0:T(256)} %refs_0_.3) | copy-start | bytes 3076
  2.3 18.8 %collective-permute-start.4 = (f32[8,8448]{1,0:T(8,128)S(1)}, f32[8,8448]{1,0:T(8,128)S(1)}, u32[]{:S(2)}, u32[]{:S(2)}) collective-permute-start(f32[8,8448]{1,0:T(8,128)S(1)} %get-tuple-element.57), channel_id=1, source_target_pairs={{0,1},{2,3},{4,5},{6,7},{8,9},{10,11},{12,13},{14,15},{16,17},{18,... | collective-permute-start | bytes 811016 | tf_op jit(solution)/shard_map/ppermute | solution.py:35
  4.2 16.9 %collective-permute-start.5 = (f32[8,4352]{1,0:T(8,128)S(1)}, f32[8,4352]{1,0:T(8,128)S(1)}, u32[]{:S(2)}, u32[]{:S(2)}) collective-permute-start(f32[8,4352]{1,0:T(8,128)S(1)} %get-tuple-element.58), channel_id=1, source_target_pairs={{1,2},{3,4},{5,6},{7,8},{9,10},{11,12},{13,14},{15,16},{17,18},{19... | collective-permute-start | bytes 417800 | tf_op jit(solution)/shard_map/ppermute | solution.py:35
  9.3 11.3 %collective-permute-start.6 = (f32[8,4096]{1,0:T(8,128)S(1)}, f32[8,4096]{1,0:T(8,128)S(1)}, u32[]{:S(2)}, u32[]{:S(2)}) collective-permute-start(f32[8,4096]{1,0:T(8,128)S(1)} %get-tuple-element.59), channel_id=1, source_target_pairs={{0,2},{1,3},{4,6},{5,7},{8,10},{9,11},{12,14},{13,15},{16,18},{17,... | collective-permute-start | bytes 393224 | tf_op jit(solution)/shard_map/ppermute | solution.py:35
  9.4 11.7 %collective-permute-start.7 = (f32[8,4096]{1,0:T(8,128)S(1)}, f32[8,4096]{1,0:T(8,128)S(1)}, u32[]{:S(2)}, u32[]{:S(2)}) collective-permute-start(f32[8,4096]{1,0:T(8,128)S(1)} %get-tuple-element.60), channel_id=1, source_target_pairs={{2,4},{3,5},{6,8},{7,9},{10,12},{11,13},{14,16},{15,17},{18,20},{1... | collective-permute-start | bytes 393224 | tf_op jit(solution)/shard_map/ppermute | solution.py:35

commit v4 on v3

--- a/solution.py
+++ b/solution.py
@@ -371,15 +371,6 @@
     parts, (home_ref, edge_ref, table_ref, _, _, coarse_ref, children_ref, parent_ref, child_ref, rim_ref, sem) = refs[:HOME], refs[HOME:]
     own, fields, _ = coarse_ref.shape
     me = lax.axis_index(AXES)
-    rims = [parts[way][:, pl.ds(ROOM[way] * CELLS, PLANE)] for way in RIMS]
-    odd = (me & 1) == 1
-    rim_ref[0] = edge_ref[0] + edge_ref[3] * jnp.where(odd, rims[0], rims[1])
-    rim_ref[1] = edge_ref[1] + edge_ref[2] * jnp.where(odd, rims[1], rims[0])
-    spots = (coarse_ref.at[0, :, pl.ds(0, PLANE)], coarse_ref.at[own - 1, :, pl.ds(CELLS - PLANE, PLANE)])
-    ends = [pltpu.make_async_copy(rim_ref.at[c], spots[c], sem.at[CAP + c]) for c in range(2)]
-    for copy in ends:
-        copy.start()
-
     def store(s, child):
         return pltpu.make_async_copy(child_ref.at[s, child], children_ref.at[s, child], sem.at[s])
 
@@ -406,6 +397,15 @@
                     child_ref[s, half * 4 + q, :, pl.ds((place + 1) * PLANE, PLANE)] = rows[x] + slope
                 for half in range(2):
                     store(s, half * 4 + q).start()
+
+    rims = [parts[way][:, pl.ds(ROOM[way] * CELLS, PLANE)] for way in RIMS]
+    odd = (me & 1) == 1
+    rim_ref[0] = edge_ref[0] + edge_ref[3] * jnp.where(odd, rims[0], rims[1])
+    rim_ref[1] = edge_ref[1] + edge_ref[2] * jnp.where(odd, rims[1], rims[0])
+    spots = (coarse_ref.at[0, :, pl.ds(0, PLANE)], coarse_ref.at[own - 1, :, pl.ds(CELLS - PLANE, PLANE)])
+    ends = [pltpu.make_async_copy(rim_ref.at[c], spots[c], sem.at[CAP + c]) for c in range(2)]
+    for copy in ends:
+        copy.start()
 
     for s in range(CAP):
         pl.when(plan_ref[s] != EMPTY)(pltpu.make_async_copy(child_ref.at[s], children_ref.at[s], sem.at[s]).wait)

time: 23.4 us -> 23.5 us (level); the launches traced: 23.2 us -> 23.1 us
  starting transfers between devices: 13.2 us -> 12.8 us
  waiting for transfers between devices: 0.55 us -> 0.82 us
    ppermute x4, starting transfers between devices: 13.2 us -> 12.8 us  [exchange(): lax.ppermute(part, AXES, pairs[way])]
    ppermute x4, waiting for transfers between devices: 0.55 us -> 0.82 us  [exchange(): lax.ppermute(part, AXES, pairs[way])]
  transfers between devices with their start and end apart: 4 -> 4, of which waited for: 1 -> 2; matrix products, arithmetic and copies ran while one was open for 0% -> 0% of each run, Pallas kernels for 22% -> 22%
where the time goes in v4:
time: 23.5 us; the launch traced here: 23.1 us
  starting transfers between devices  12.8 us (54%)
  Pallas kernels  8.77 us (37%)
  waiting for transfers between devices  0.82 us (3%)
  between operations  0.71 us (3%)
    ppermute x4, starting transfers between devices, exchange(): lax.ppermute(part, AXES, pairs[way])  12.8 us
    pallas_call x1, Pallas kernels, coarse(): pl.pallas_call(coarse_kernel, out_shape=[pltpu.HBM(cons.shape, jnp.float3...  5.05 us
    pallas_call x1, Pallas kernels, unpack(): pl.pallas_call(unpack_kernel, out_shape=[pltpu.HBM(stepped.shape, jnp.flo...  2.1 us
    pallas_call x1, Pallas kernels, pack(): pl.pallas_call(functools.partial(pack_kernel, later), out_shape=[jax.Shap...  1.61 us
    ppermute x4, waiting for transfers between devices, exchange(): lax.ppermute(part, AXES, pairs[way])  0.82 us
  transfers between devices with their start and end apart: 4, of which 2 were waited for; matrix products, arithmetic and copies ran while one was open for 0% of the time, Pallas kernels for 22%

profile of v4, /device:TPU:96, one launch (start us, length us, event | category | flops | bytes accessed | tf_op | source)
XLA Modules:
  0.0 23.1 jit_solution(13422490253271692236)
XLA Ops:
  0.6 0.0 copy-start.1
  0.6 0.0 copy-start
  0.7 1.6 %pack.2 = (f32[8,8448]{1,0:T(8,128)S(1)}, f32[8,4352]{1,0:T(8,128)S(1)}, f32[8,4096]{1,0:T(8,128)S(1)}, f32[8,4096]{1,0:T(8,128)S(1)}) custom-call(s32[256]{0:T(256)} %refs_0_.3, s32[256]{0:T(256)} %refs_1_.3, f32[32,8,4096]{2,1,0:T(8,128)} %refs_2_.3), custom_call_target="tpu_custom_call" | custom-call | bytes 1048576 | tf_op jit(solution)/shard_map/pack/pallas_call | solution.py:153
  2.3 1.9 %collective-permute-start.4 = (f32[8,8448]{1,0:T(8,128)S(1)}, f32[8,8448]{1,0:T(8,128)S(1)}, u32[]{:S(2)}, u32[]{:S(2)}) collective-permute-start(f32[8,8448]{1,0:T(8,128)S(1)} %get-tuple-element.57), channel_id=1, source_target_pairs={{0,1},{2,3},{4,5},{6,7},{8,9},{10,11},{12,13},{14,15},{16,17},{18,... | collective-permute-start | bytes 811016 | tf_op jit(solution)/shard_map/ppermute | solution.py:35
  4.2 5.5 %collective-permute-start.5 = (f32[8,4352]{1,0:T(8,128)S(1)}, f32[8,4352]{1,0:T(8,128)S(1)}, u32[]{:S(2)}, u32[]{:S(2)}) collective-permute-start(f32[8,4352]{1,0:T(8,128)S(1)} %get-tuple-element.58), channel_id=1, source_target_pairs={{1,2},{3,4},{5,6},{7,8},{9,10},{11,12},{13,14},{15,16},{17,18},{19... | collective-permute-start | bytes 417800 | tf_op jit(solution)/shard_map/ppermute | solution.py:35
  9.7 0.1 collective-permute-start.6
  9.8 5.3 %collective-permute-start.7 = (f32[8,4096]{1,0:T(8,128)S(1)}, f32[8,4096]{1,0:T(8,128)S(1)}, u32[]{:S(2)}, u32[]{:S(2)}) collective-permute-start(f32[8,4096]{1,0:T(8,128)S(1)} %get-tuple-element.60), channel_id=1, source_target_pairs={{2,4},{3,5},{6,8},{7,9},{10,12},{11,13},{14,16},{15,17},{18,20},{1... | collective-permute-start | bytes 393224 | tf_op jit(solution)/shard_map/ppermute | solution.py:35
  15.1 5.1 %coarse.1 = (f32[32,8,4096]{2,1,0:T(8,128)}, f32[3,8,8,4096]{3,2,1,0:T(8,128)}, f32[4,8,256]{2,1,0:T(8,128)S(1)}, bf16[256,1024]{1,0:T(8,128)(2,1)S(1)}, f32[3,8...) custom-call(s32[256]{0:T(256)} %refs_0_.3, s32[256]{0:T(256)} %refs_1_.3, f32[8]{0:T(128)} %refs_2_.2, f32[8]{0:T(128)} %refs_3_.1, ...), custom_call_target="tpu_custom_call" | custom-call | flops 1073741824 | bytes 8388608 | tf_op jit(solution)/shard_map/coarse/pallas_call | solution.py:312
  20.2 0.0 collective-permute-done.6.refs_2_
  20.2 0.6 %collective-permute-done.7.refs_3_ = f32[8,4096]{1,0:T(8,128)S(1)} collective-permute-done((f32[8,4096]{1,0:T(8,128)S(1)}, f32[8,4096]{1,0:T(8,128)S(1)}, u32[]{:S(2)}, u32[]{:S(2)}) %collective-permute-start.7) | collective-permute-done | bytes 131104 | tf_op jit(solution)/shard_map/ppermute | solution.py:35
  20.8 0.2 collective-permute-done.5.refs_1_
  21.0 0.0 collective-permute-done.4.refs_0_
  21.0 0.0 copy-done.1
  21.0 0.0 copy-done
  21.0 2.1 %unpack.1 = (f32[32,8,4096]{2,1,0:T(8,128)}, f32[3,8,8,4096]{3,2,1,0:T(8,128)}) custom-call(s32[3]{0:T(128)S(4)} %get-tuple-element.55.plan_ref, f32[8,8448]{1,0:T(8,128)S(1)} %collective-permute-done.4.refs_0_, f32[8,4352]{1,0:T(8,128)S(1)} %collective-permute-done.5.refs_1_, ...), custom_call_target="tpu_custom_call", output_to_operand_aliasing={{0}: (8, {}), {1}: (9, {})} | custom-call | flops 402653184 | bytes 5242880 | tf_op jit(solution)/shard_map/unpack/pallas_call | solution.py:422
  (1 shorter events, 0.0 us)
Async XLA Ops:
  0.6 20.4 %copy-start.1 = (s32[256]{0:T(256)S(1)}, s32[256]{0:T(256)}, u32[]{:S(2)}) copy-start(s32[256]{0:T(256)} %refs_1_.3) | copy-start | bytes 3076
  0.6 20.3 %copy-start = (s32[256]{0:T(256)S(1)}, s32[256]{0:T(256)}, u32[]{:S(2)}) copy-start(s32[256]{0:T(256)} %refs_0_.3) | copy-start | bytes 3076
  2.3 18.7 %collective-permute-start.4 = (f32[8,8448]{1,0:T(8,128)S(1)}, f32[8,8448]{1,0:T(8,128)S(1)}, u32[]{:S(2)}, u32[]{:S(2)}) collective-permute-start(f32[8,8448]{1,0:T(8,128)S(1)} %get-tuple-element.57), channel_id=1, source_target_pairs={{0,1},{2,3},{4,5},{6,7},{8,9},{10,11},{12,13},{14,15},{16,17},{18,... | collective-permute-start | bytes 811016 | tf_op jit(solution)/shard_map/ppermute | solution.py:35
  4.2 16.8 %collective-permute-start.5 = (f32[8,4352]{1,0:T(8,128)S(1)}, f32[8,4352]{1,0:T(8,128)S(1)}, u32[]{:S(2)}, u32[]{:S(2)}) collective-permute-start(f32[8,4352]{1,0:T(8,128)S(1)} %get-tuple-element.58), channel_id=1, source_target_pairs={{1,2},{3,4},{5,6},{7,8},{9,10},{11,12},{13,14},{15,16},{17,18},{19... | collective-permute-start | bytes 417800 | tf_op jit(solution)/shard_map/ppermute | solution.py:35
  9.7 10.5 %collective-permute-start.6 = (f32[8,4096]{1,0:T(8,128)S(1)}, f32[8,4096]{1,0:T(8,128)S(1)}, u32[]{:S(2)}, u32[]{:S(2)}) collective-permute-start(f32[8,4096]{1,0:T(8,128)S(1)} %get-tuple-element.59), channel_id=1, source_target_pairs={{0,2},{1,3},{4,6},{5,7},{8,10},{9,11},{12,14},{13,15},{16,18},{17,... | collective-permute-start | bytes 393224 | tf_op jit(solution)/shard_map/ppermute | solution.py:35
  9.8 11.0 %collective-permute-start.7 = (f32[8,4096]{1,0:T(8,128)S(1)}, f32[8,4096]{1,0:T(8,128)S(1)}, u32[]{:S(2)}, u32[]{:S(2)}) collective-permute-start(f32[8,4096]{1,0:T(8,128)S(1)} %get-tuple-element.60), channel_id=1, source_target_pairs={{2,4},{3,5},{6,8},{7,9},{10,12},{11,13},{14,16},{15,17},{18,20},{1... | collective-permute-start | bytes 393224 | tf_op jit(solution)/shard_map/ppermute | solution.py:35
